TPU v7x, 128 devices: a whole 4x4x4 slice. The times are simulated.
128 devices in a mesh: layer: 4 (over x), trace: 32 (over z, y, core).
Axes of the slice: x: 4, y: 4, z: 4, core: 2. Of those that a mesh axis runs over, the one named last changes fastest.
Arguments:
- operators: bfloat16 [4, 768, 512, 512], P('layer', 'trace'), may hold values from -0.15625 to 0.15625
- sources: bfloat16 [4, 2, 131072, 128], P('layer', None, 'trace'), may hold values from -6 to 6
- row_block: int32 [4, 32, 24], P('layer'), may hold values from 0 to 255, as said below
- col_block: int32 [4, 32, 24], P('layer', 'trace'), may hold values from 0 to 255, as said below
Outputs:
- traces: bfloat16 [4, 2, 131072, 128], P('layer', None, 'trace')
Inputs may be any that keep to these rules, and one draw needn't show every extreme that they name: `row_block`: for each layer and each trace index d, the 24 row blocks name distinct owners; in each layer some owner is named by every d, and so are owners 0 and 31. `col_block`: entries of trace index d lie in d * 8 to (d + 1) * 8 - 1.
All inputs are finite; a program needn't handle non-finite values.
Results may differ from a plain program's by a relative error of at most 0.0077.
Values may be sent and summed in bfloat16 or wider, within the bound.
A program may use at most 128 MiB of HBM per device.

v0:
```python
import jax
import jax.numpy as jnp
from jax import lax
from jax.sharding import PartitionSpec as P

BATCHES = 2


def passed_along(value, axis, steps):
    count = lax.axis_size(axis)
    initial, last = (max(0, -steps), min(count, count - steps))
    return lax.ppermute(value, axis, [(source, source + steps) for source in range(initial, last)])


def body(operators, sources, row_block, col_block):
    position = lax.axis_index("trace")
    senders = lax.axis_size("trace")
    blocks = operators[0]
    rows_all = row_block[0]
    my_sources = sources[0]
    width = blocks.shape[-1]
    owned = my_sources.shape[1] // width
    stored = blocks.shape[0]
    my_rows = lax.dynamic_index_in_dim(rows_all, position, 0, keepdims=False)
    my_cols = col_block[0, 0] - position * owned
    targets = my_rows // owned
    match_send = targets[None, :] == jnp.arange(senders)[:, None]
    slot_index = jnp.sum(jnp.where(match_send, jnp.arange(stored)[None, :], 0), axis=1)
    slot_used = jnp.any(match_send, axis=1).astype(jnp.bfloat16)
    mine = rows_all // owned == position
    local_rows = rows_all % owned
    hits = mine[None, :, :] & (local_rows[None, :, :] == jnp.arange(owned)[:, None, None])
    selector = jnp.sum(hits.astype(jnp.float32), axis=2).astype(jnp.bfloat16)
    layers = lax.axis_size("layer")
    shots = my_sources.shape[2]
    depth = lax.axis_index("layer")
    traces = jnp.zeros(my_sources.shape, jnp.bfloat16)
    incoming = jnp.zeros((owned * width, shots), jnp.bfloat16)
    total_steps = layers + BATCHES - 1
    for section in range(total_steps):
        which = section - depth
        valid = (which >= 0) & (which < BATCHES)
        clipped = jnp.clip(which, 0, BATCHES - 1)
        source = lax.dynamic_index_in_dim(my_sources, clipped, 0, keepdims=False)
        field = (incoming.astype(jnp.float32) + source.astype(jnp.float32)).astype(jnp.bfloat16)
        products_columns = field.shape[1]
        tiles = field.reshape(owned, width, products_columns)
        pieces = tiles[my_cols]
        prod = jnp.einsum(
            "kij,kjc->kic", blocks, pieces, preferred_element_type=jnp.float32
        ).astype(jnp.bfloat16)
        received = lax.all_to_all(
            prod[slot_index] * slot_used[:, None, None],
            "trace",
            split_axis=0,
            concat_axis=0,
            tiled=True,
        )
        columns = received.shape[2]
        summed = jnp.einsum("rs,sic->ric", selector, received, preferred_element_type=jnp.float32)
        outgoing = summed.reshape(owned * width, columns).astype(jnp.bfloat16)
        current = lax.dynamic_index_in_dim(traces, clipped, 0, keepdims=False)
        traces = lax.dynamic_update_index_in_dim(
            traces, jnp.where(valid, outgoing, current), clipped, 0
        )
        if section + 1 < total_steps:
            incoming = passed_along(outgoing, "layer", 1)
    return traces[None]


def solution(mesh):
    placed = (
        P("layer", "trace", None, None),
        P("layer", None, "trace", None),
        P("layer", None, None),
        P("layer", "trace", None),
    )
    return jax.shard_map(
        body, mesh=mesh, in_specs=placed, out_specs=P("layer", None, "trace", None), check_vma=False
    )
```

profile of v0, /device:TPU:7, one launch (start us, length us, event | category | flops | bytes accessed | tf_op | source)
XLA Modules:
  0.0 537.7 jit_solution(9775520468814412415)
XLA Ops:
  3.1 2.7 gather_fusion
  5.7 11.5 %convert_bitcast_fusion.4 = bf16[24,512,128]{1,2,0:T(8,128)(2,1)} fusion(bf16[24,512,128]{2,1,0:T(8,128)(2,1)} %gather_fusion, bf16[1,24,512,512]{3,2,1,0:T(8,128)(2,1)} %param.4), kind=kOutput, calls=%fused_computation.34 | convolution fusion | flops 1612185600 | bytes 18874368 | tf_op jit(solution)/shard_map/kij,kjc->kic/dot_general | solution.py:49
  17.2 3.5 copy.71
  20.7 3.1 gather_fusion.1
  23.8 4.5 broadcast_multiply_fusion.4
  28.3 9.0 %all-to-all-start = ((bf16[32,512,128]{2,1,0:T(8,128)(2,1)}), bf16[32,512,128]{2,1,0:T(8,128)(2,1)}, u32[]{:S(2)}, u32[]{:S(2)}) async-start(bf16[32,512,128]{2,1,0:T(8,128)(2,1)} %broadcast_multiply_fusion.4), calls=%async_computation | async-start | bytes 8388608 | tf_op jit(solution)/shard_map/all_to_all | solution.py:52
  37.4 50.2 %all-to-all-done = bf16[32,512,128]{2,1,0:T(8,128)(2,1)} async-done(((bf16[32,512,128]{2,1,0:T(8,128)(2,1)}), bf16[32,512,128]{2,1,0:T(8,128)(2,1)}, u32[]{:S(2)}, u32[]{:S(2)}) %all-to-all-start) | async-done | bytes 4194336 | tf_op jit(solution)/shard_map/all_to_all | solution.py:52
  87.5 5.5 %broadcast_select_fusion = (bf16[8,512,128]{2,0,1:T(8,128)(2,1)}, bf16[8,512,128]{2,0,1:T(8,128)(2,1)S(1)}) fusion(pred[]{:T(512)S(6)} %and.53, bf16[32,512,128]{2,1,0:T(8,128)(2,1)} %all-to-all-done, bf16[8,32]{1,0:T(8,128)(2,1)S(1)} %convert_reduce_fusion), kind=kOutput, calls=%fused_computation.62 | convolution fusion | flops 34603008 | bytes 6291969 | tf_op jit(solution)/shard_map/rs,sic->ric/dot_general | solution.py:60
  95.1 21.3 %collective-permute-done = bf16[4096,128]{1,0:T(8,128)(2,1)} collective-permute-done((bf16[4096,128]{1,0:T(8,128)(2,1)S(1)}, bf16[4096,128]{1,0:T(8,128)(2,1)}, u32[]{:S(2)}, u32[]{:S(2)}) %collective-permute-start) | collective-permute-done | bytes 1048608 | tf_op jit(solution)/shard_map/ppermute | solution.py:12
  120.5 11.5 %convert_bitcast_fusion.3 = bf16[24,512,128]{1,2,0:T(8,128)(2,1)} fusion(bf16[24,512,128]{2,1,0:T(8,128)(2,1)} %gather_fusion.2, bf16[1,24,512,512]{3,2,1,0:T(8,128)(2,1)} %param.4), kind=kOutput, calls=%fused_computation.33 | convolution fusion | flops 1612185600 | bytes 18874368 | tf_op jit(solution)/shard_map/kij,kjc->kic/dot_general | solution.py:49
  132.0 3.5 copy.76
  135.5 3.0 gather_fusion.3
  141.1 60.5 %all_to_all.25 = bf16[32,512,128]{2,1,0:T(8,128)(2,1)S(1)} all-to-all(bf16[32,512,128]{2,1,0:T(8,128)(2,1)S(1)} %broadcast_multiply_fusion.3), channel_id=1, replica_groups=mesh['layer'=4,'trace'=32] {'trace'}, dimensions={0} | all-to-all | bytes 8388608 | tf_op jit(solution)/shard_map/all_to_all | solution.py:52
  205.6 24.9 %collective-permute-done.1 = bf16[4096,128]{1,0:T(8,128)(2,1)} collective-permute-done((bf16[4096,128]{1,0:T(8,128)(2,1)S(1)}, bf16[4096,128]{1,0:T(8,128)(2,1)}, u32[]{:S(2)}, u32[]{:S(2)}) %collective-permute-start.1) | collective-permute-done | bytes 1048608 | tf_op jit(solution)/shard_map/ppermute | solution.py:12
  232.0 2.7 gather_fusion.4
  234.6 11.5 %convert_bitcast_fusion.2 = bf16[24,512,128]{1,2,0:T(8,128)(2,1)} fusion(bf16[24,512,128]{2,1,0:T(8,128)(2,1)} %gather_fusion.4, bf16[1,24,512,512]{3,2,1,0:T(8,128)(2,1)} %param.4), kind=kOutput, calls=%fused_computation.32 | convolution fusion | flops 1612185600 | bytes 18874368 | tf_op jit(solution)/shard_map/kij,kjc->kic/dot_general | solution.py:49
  246.1 3.5 copy.81
  249.6 3.0 gather_fusion.5
  255.2 55.5 %all_to_all.26 = bf16[32,512,128]{2,1,0:T(8,128)(2,1)S(1)} all-to-all(bf16[32,512,128]{2,1,0:T(8,128)(2,1)S(1)} %broadcast_multiply_fusion.2), channel_id=1, replica_groups=mesh['layer'=4,'trace'=32] {'trace'}, dimensions={0} | all-to-all | bytes 8388608 | tf_op jit(solution)/shard_map/all_to_all | solution.py:52
  314.7 24.8 %collective-permute-done.2 = bf16[4096,128]{1,0:T(8,128)(2,1)} collective-permute-done((bf16[4096,128]{1,0:T(8,128)(2,1)S(1)}, bf16[4096,128]{1,0:T(8,128)(2,1)}, u32[]{:S(2)}, u32[]{:S(2)}) %collective-permute-start.2) | collective-permute-done | bytes 1048608 | tf_op jit(solution)/shard_map/ppermute | solution.py:12
  343.7 11.5 %convert_bitcast_fusion.1 = bf16[24,512,128]{1,2,0:T(8,128)(2,1)} fusion(bf16[24,512,128]{2,1,0:T(8,128)(2,1)} %gather_fusion.6, bf16[1,24,512,512]{3,2,1,0:T(8,128)(2,1)} %param.4), kind=kOutput, calls=%fused_computation.31 | convolution fusion | flops 1612185600 | bytes 18874368 | tf_op jit(solution)/shard_map/kij,kjc->kic/dot_general | solution.py:49
  355.2 3.5 copy.86
  358.7 3.0 gather_fusion.7
  364.3 55.5 %all_to_all.27 = bf16[32,512,128]{2,1,0:T(8,128)(2,1)S(1)} all-to-all(bf16[32,512,128]{2,1,0:T(8,128)(2,1)S(1)} %broadcast_multiply_fusion.1), channel_id=1, replica_groups=mesh['layer'=4,'trace'=32] {'trace'}, dimensions={0} | all-to-all | bytes 8388608 | tf_op jit(solution)/shard_map/all_to_all | solution.py:52
  423.8 24.8 %collective-permute-done.3 = bf16[4096,128]{1,0:T(8,128)(2,1)} collective-permute-done((bf16[4096,128]{1,0:T(8,128)(2,1)S(1)}, bf16[4096,128]{1,0:T(8,128)(2,1)}, u32[]{:S(2)}, u32[]{:S(2)}) %collective-permute-start.3) | collective-permute-done | bytes 1048608 | tf_op jit(solution)/shard_map/ppermute | solution.py:12
  452.8 11.5 %convert_bitcast_fusion = bf16[24,512,128]{1,2,0:T(8,128)(2,1)} fusion(bf16[24,512,128]{2,1,0:T(8,128)(2,1)} %gather_fusion.8, bf16[1,24,512,512]{3,2,1,0:T(8,128)(2,1)} %param.4), kind=kOutput, calls=%fused_computation.30 | convolution fusion | flops 1612185600 | bytes 18874368 | tf_op jit(solution)/shard_map/kij,kjc->kic/dot_general | solution.py:49
  464.3 3.5 copy.91
  467.8 3.1 gather_fusion.9
  470.8 4.5 broadcast_multiply_fusion
  475.3 5.8 %all-to-all-start.4 = ((bf16[32,512,128]{2,1,0:T(8,128)(2,1)}), bf16[32,512,128]{2,1,0:T(8,128)(2,1)}, u32[]{:S(2)}, u32[]{:S(2)}) async-start(bf16[32,512,128]{2,1,0:T(8,128)(2,1)} %broadcast_multiply_fusion), calls=%async_computation.4 | async-start | bytes 8388608 | tf_op jit(solution)/shard_map/all_to_all | solution.py:52
  485.4 46.2 %all-to-all-done.4 = bf16[32,512,128]{2,1,0:T(8,128)(2,1)} async-done(((bf16[32,512,128]{2,1,0:T(8,128)(2,1)}), bf16[32,512,128]{2,1,0:T(8,128)(2,1)}, u32[]{:S(2)}, u32[]{:S(2)}) %all-to-all-start.4) | async-done | bytes 4194336 | tf_op jit(solution)/shard_map/all_to_all | solution.py:52
  531.5 4.5 fusion.46
  (67 shorter events, 44.3 us)
Async XLA Ops:
  28.3 9.0 %copy-start.11 = (s32[1,32,24]{1,2,0:T(8,128)S(1)}, s32[1,32,24]{1,2,0:T(8,128)}, u32[]{:S(2)}) copy-start(s32[1,32,24]{1,2,0:T(8,128)} %param.6) | copy-start | bytes 9220
  28.3 59.2 %all-to-all-start = ((bf16[32,512,128]{2,1,0:T(8,128)(2,1)}), bf16[32,512,128]{2,1,0:T(8,128)(2,1)}, u32[]{:S(2)}, u32[]{:S(2)}) async-start(bf16[32,512,128]{2,1,0:T(8,128)(2,1)} %broadcast_multiply_fusion.4), calls=%async_computation | async-start | bytes 8388608 | tf_op jit(solution)/shard_map/all_to_all | solution.py:52
  37.4 79.0 %copy-start = (bf16[1,2,4096,128]{3,2,1,0:T(8,128)(2,1)S(1)}, bf16[1,2,4096,128]{3,2,1,0:T(8,128)(2,1)}, u32[]{:S(2)}) copy-start(bf16[1,2,4096,128]{3,2,1,0:T(8,128)(2,1)} %param.5) | copy-start | bytes 6291460
  93.2 23.1 %collective-permute-start = (bf16[4096,128]{1,0:T(8,128)(2,1)S(1)}, bf16[4096,128]{1,0:T(8,128)(2,1)}, u32[]{:S(2)}, u32[]{:S(2)}) collective-permute-start(bf16[4096,128]{1,0:T(8,128)(2,1)S(1)} %bitcast.122), channel_id=1, source_target_pairs={{0,32},{32,64},{64,96},{1,33},{33,65},{65,97},{2,34},{34,66},{66,9... | collective-permute-start | bytes 3145736 | tf_op jit(solution)/shard_map/ppermute | solution.py:12
  201.6 28.9 %copy-start.1 = (bf16[1,2,4096,128]{3,2,1,0:T(8,128)(2,1)S(1)}, bf16[1,2,4096,128]{3,2,1,0:T(8,128)(2,1)}, u32[]{:S(2)}) copy-start(bf16[1,2,4096,128]{3,2,1,0:T(8,128)(2,1)} %param.5) | copy-start | bytes 6291460
  204.1 1.5 copy-start.4
  204.1 26.3 %collective-permute-start.1 = (bf16[4096,128]{1,0:T(8,128)(2,1)S(1)}, bf16[4096,128]{1,0:T(8,128)(2,1)}, u32[]{:S(2)}, u32[]{:S(2)}) collective-permute-start(bf16[4096,128]{1,0:T(8,128)(2,1)S(1)} %bitcast.115), channel_id=1, source_target_pairs={{0,32},{32,64},{64,96},{1,33},{33,65},{65,97},{2,34},{34,66},{66,9... | collective-permute-start | bytes 3145736 | tf_op jit(solution)/shard_map/ppermute | solution.py:12
  310.7 28.9 %copy-start.2 = (bf16[1,2,4096,128]{3,2,1,0:T(8,128)(2,1)S(1)}, bf16[1,2,4096,128]{3,2,1,0:T(8,128)(2,1)}, u32[]{:S(2)}) copy-start(bf16[1,2,4096,128]{3,2,1,0:T(8,128)(2,1)} %param.5) | copy-start | bytes 6291460
  313.2 1.5 copy-start.6
  313.2 26.3 %collective-permute-start.2 = (bf16[4096,128]{1,0:T(8,128)(2,1)S(1)}, bf16[4096,128]{1,0:T(8,128)(2,1)}, u32[]{:S(2)}, u32[]{:S(2)}) collective-permute-start(bf16[4096,128]{1,0:T(8,128)(2,1)S(1)} %bitcast.117), channel_id=1, source_target_pairs={{0,32},{32,64},{64,96},{1,33},{33,65},{65,97},{2,34},{34,66},{66,9... | collective-permute-start | bytes 3145736 | tf_op jit(solution)/shard_map/ppermute | solution.py:12
  419.8 28.9 %copy-start.3 = (bf16[1,2,4096,128]{3,2,1,0:T(8,128)(2,1)S(1)}, bf16[1,2,4096,128]{3,2,1,0:T(8,128)(2,1)}, u32[]{:S(2)}) copy-start(bf16[1,2,4096,128]{3,2,1,0:T(8,128)(2,1)} %param.5) | copy-start | bytes 6291460
  422.3 1.6 copy-start.8
  422.3 26.3 %collective-permute-start.3 = (bf16[4096,128]{1,0:T(8,128)(2,1)S(1)}, bf16[4096,128]{1,0:T(8,128)(2,1)}, u32[]{:S(2)}, u32[]{:S(2)}) collective-permute-start(bf16[4096,128]{1,0:T(8,128)(2,1)S(1)} %bitcast.119), channel_id=1, source_target_pairs={{0,32},{32,64},{64,96},{1,33},{33,65},{65,97},{2,34},{34,66},{66,9... | collective-permute-start | bytes 3145736 | tf_op jit(solution)/shard_map/ppermute | solution.py:12
  475.3 5.8 %copy-start.10 = (bf16[8,512,128]{2,0,1:T(8,128)(2,1)S(1)}, bf16[8,512,128]{2,0,1:T(8,128)(2,1)}, u32[]{:S(2)}) copy-start(bf16[8,512,128]{2,0,1:T(8,128)(2,1)} %get-tuple-element.5) | copy-start | bytes 3145732
  475.3 56.2 %all-to-all-start.4 = ((bf16[32,512,128]{2,1,0:T(8,128)(2,1)}), bf16[32,512,128]{2,1,0:T(8,128)(2,1)}, u32[]{:S(2)}, u32[]{:S(2)}) async-start(bf16[32,512,128]{2,1,0:T(8,128)(2,1)} %broadcast_multiply_fusion), calls=%async_computation.4 | async-start | bytes 8388608 | tf_op jit(solution)/shard_map/all_to_all | solution.py:52
  481.2 1.2 copy-start.5
  481.6 1.3 copy-start.7
  482.4 1.3 copy-start.9
where the time goes:
time: 548 us; the launch traced here: 538 us
  waiting for transfers between devices  192 us (35%)
  blocking collectives  172 us (31%)
  matrix products  74.5 us (14%)
  local copies, waits for them, and re-layouts  52.1 us (10%)
  other arithmetic  25.8 us (5%)
  starting transfers between devices  21.1 us (4%)
    all_to_all x3, blocking collectives, body(): lax.all_to_all(prod[slot_index] * slot_used[:, None, None], 'trace', spli...  172 us
    all_to_all x2, waiting for transfers between devices, body(): lax.all_to_all(prod[slot_index] * slot_used[:, None, None], 'trace', spli...  96.3 us
    ppermute x4, waiting for transfers between devices, passed_along(): lax.ppermute(value, axis, [(source, source + steps) for source in range(i...  95.7 us
    dot_general x5, matrix products, body(): jnp.einsum('kij,kjc->kic', blocks, pieces, preferred_element_type=jnp.flo...  57.4 us
    convert_element_type x5, local copies, waits for them, and re-layouts, body(): prod = jnp.einsum('kij,kjc->kic', blocks, pieces, preferred_element_type=...  17.4 us
    dot_general x5, matrix products, body(): jnp.einsum('rs,sic->ric', selector, received, preferred_element_type=jnp....  17.1 us
    mul x5, other arithmetic, body(): prod[slot_index] * slot_used[:, None, None]  16.6 us
    gather x5, local copies, waits for them, and re-layouts, body(): prod[slot_index] * slot_used[:, None, None]  15.2 us
  transfers between devices with their start and end apart: 6, of which 6 were waited for; matrix products, arithmetic and copies ran while one was open for 1% of the time, Pallas kernels for 0%

commit v1 on v0

v1 whole, which is shorter than its diff:
```python
import functools

import jax
import jax.numpy as jnp
from jax import lax
from jax.experimental import pallas as pl
from jax.experimental.pallas import tpu as pltpu
from jax.sharding import PartitionSpec as P

MESH = pl.DeviceIdType.MESH
CHUNK = 16
PIECES = 2


def displacements(senders):
    side = 4 if senders == 32 else 2
    if side == 2:
        steps = [(1, 1), (1, 0), (0, 1)]
    else:
        steps = [(2, 2)]
        steps += [(2, 1), (1, 2), (2, 3), (3, 2)]
        steps += [(1, 1), (3, 1), (3, 3), (1, 3)]
        steps += [(2, 0), (0, 2)]
        steps += [(1, 0), (0, 1), (3, 0), (0, 3)]
    order, seen = [], set()
    for a, b in steps:
        kind = tuple(sorted((min(a, side - a), min(b, side - b))))
        if kind in seen:
            continue
        seen.add(kind)
        alike = [s for s in steps if tuple(sorted((min(s[0], side - s[0]), min(s[1], side - s[1])))) == kind]
        order += [(p, q, core) for core in range(2) for p, q in alike]
    return side, order + [(0, 0, 1)]


def sweep(
    side, order, table, operators, sources, out, blocks, field, sent, got, incoming,
    load_sem, send_sem, recv_sem, down_sem, arrive_sem,
):
    chunks, wide, rows = sources.shape
    stored, width, _ = blocks.shape
    owned = rows // width
    peers = len(order)
    part = owned // PIECES
    depth = lax.axis_index("layer")
    layers = lax.axis_size("layer")
    me = lax.axis_index("trace")
    z, y, core = me // (2 * side), (me // 2) % side, me % 2

    def at(step, sign):
        a, b, c = step
        return ((z + sign * a + side) % side) * (2 * side) + ((y + sign * b + side) % side) * 2 + (core + c) % 2

    load = pltpu.make_async_copy(operators, blocks, load_sem)
    load.start()
    barrier = pltpu.get_barrier_semaphore()
    for step in order:
        pl.semaphore_signal(barrier, inc=1, device_id=(depth, at(step, -1)), device_id_type=MESH)

    pl.semaphore_signal(
        barrier, inc=1, device_id=(lax.rem(depth + layers - 1, layers), me), device_id_type=MESH
    )
    pl.semaphore_wait(barrier, peers + 1)
    load.wait()

    def to_peer(k, i):
        return pltpu.make_async_remote_copy(
            src_ref=sent.at[k, i], dst_ref=got.at[k, i], send_sem=send_sem.at[k], recv_sem=recv_sem.at[k],
            device_id=(depth, at(order[i], 1)), device_id_type=MESH,
        )

    def all_peers(k):
        return pltpu.make_async_remote_copy(
            src_ref=sent.at[k], dst_ref=got.at[k, pl.ds(0, peers)], send_sem=send_sem.at[k],
            recv_sem=recv_sem.at[k], device_id=(depth, at(order[0], 1)), device_id_type=MESH,
        )

    def down(k, p):
        span = pl.ds(p * part * width, part * width)
        return pltpu.make_async_remote_copy(
            src_ref=out.at[k, :, span], dst_ref=incoming.at[k, :, span], send_sem=down_sem.at[k, p],
            recv_sem=arrive_sem.at[k, p], device_id=(lax.rem(depth + 1, layers), me), device_id_type=MESH,
        )

    def multiply(k):
        @pl.when(depth > 0)
        def _():
            for p in range(PIECES):
                down(k, p).wait_recv()

        for c in range(owned):
            span = pl.ds(c * width, width)
            above = jnp.where(depth > 0, incoming[k, :, span].astype(jnp.float32), 0.0)
            field[c] = (above + sources[k, :, span].astype(jnp.float32)).astype(jnp.bfloat16)
        for i in range(peers + 1):
            owner = at(order[i], 1) if i < peers else me
            product = lax.dot_general(
                field[table[1, owner]], blocks[table[0, owner]], (((1,), (1,)), ((), ())),
                preferred_element_type=jnp.float32,
            ).astype(jnp.bfloat16)
            if i < peers:
                sent[k, i] = product
                to_peer(k, i).start()
            else:
                got[k, i] = product

    def collect(k):
        all_peers(k).wait_recv()
        local = [table[2, at(order[i], -1) if i < peers else me] for i in range(peers + 1)]
        for p in range(PIECES):
            for r in range(p * part, (p + 1) * part):
                total = jnp.zeros((wide, width), jnp.float32)
                for i in range(peers + 1):
                    pick = jnp.where(local[i] == r, 1.0, 0.0)
                    total += got[k, i].astype(jnp.float32) * pick
                out[k, :, pl.ds(r * width, width)] = total.astype(jnp.bfloat16)

            @pl.when(depth < layers - 1)
            def _():
                down(k, p).start()

    def turn(k, _):
        @pl.when(k < chunks)
        def _():
            multiply(k)

        @pl.when(k > 0)
        def _():
            collect(k - 1)

        return 0

    lax.fori_loop(0, chunks + 1, turn, 0)

    def finish(k, _):
        all_peers(k).wait_send()

        @pl.when(depth < layers - 1)
        def _():
            for p in range(PIECES):
                down(k, p).wait_send()

        return 0

    lax.fori_loop(0, chunks, finish, 0)


def body(operators, sources, row_block, col_block):
    position = lax.axis_index("trace")
    senders = lax.axis_size("trace")
    blocks = operators[0]
    stored, width, _ = blocks.shape
    batches, rows, shots = sources.shape[1:]
    owned = rows // width
    side, order = displacements(senders)
    every = row_block[0]
    my_rows = lax.dynamic_index_in_dim(every, position, 0, keepdims=False)
    my_cols = col_block[0, 0] - position * owned
    match = (my_rows // owned)[None, :] == jnp.arange(senders)[:, None]
    slot = jnp.sum(jnp.where(match, jnp.arange(stored)[None, :], 0), axis=1)
    column = jnp.sum(jnp.where(match, my_cols[None, :], 0), axis=1)
    mine = every // owned == position
    local = jnp.sum(jnp.where(mine, every % owned + 1, 0), axis=1) - 1
    table = jnp.stack([slot, column, local]).astype(jnp.int32)
    chunks = batches * shots // CHUNK
    turned = jnp.swapaxes(sources[0], 1, 2).reshape(chunks, CHUNK, rows)
    peers = len(order)
    result = pl.pallas_call(
        functools.partial(sweep, side, order),
        out_shape=jax.ShapeDtypeStruct((chunks, CHUNK, rows), jnp.bfloat16),
        in_specs=[
            pl.BlockSpec(memory_space=pltpu.SMEM),
            pl.BlockSpec(memory_space=pl.ANY),
            pl.BlockSpec(memory_space=pltpu.VMEM),
        ],
        out_specs=pl.BlockSpec(memory_space=pltpu.VMEM),
        scratch_shapes=[
            pltpu.VMEM((stored, width, width), jnp.bfloat16),
            pltpu.VMEM((owned, CHUNK, width), jnp.bfloat16),
            pltpu.VMEM((chunks, peers, CHUNK, width), jnp.bfloat16),
            pltpu.VMEM((chunks, peers + 1, CHUNK, width), jnp.bfloat16),
            pltpu.VMEM((chunks, CHUNK, rows), jnp.bfloat16),
            pltpu.SemaphoreType.DMA,
            pltpu.SemaphoreType.DMA((chunks,)),
            pltpu.SemaphoreType.DMA((chunks,)),
            pltpu.SemaphoreType.DMA((chunks, PIECES)),
            pltpu.SemaphoreType.DMA((chunks, PIECES)),
        ],
        compiler_params=pltpu.CompilerParams(
            collective_id=0, has_side_effects=True, vmem_limit_bytes=56 * 1024 * 1024
        ),
        name="sweep",
    )(table, blocks, turned)
    return jnp.swapaxes(result.reshape(batches, shots, rows), 1, 2)[None]


def solution(mesh):
    placed = (
        P("layer", "trace", None, None),
        P("layer", None, "trace", None),
        P("layer", None, None),
        P("layer", "trace", None),
    )
    return jax.shard_map(
        body, mesh=mesh, in_specs=placed, out_specs=P("layer", None, "trace", None), check_vma=False
    )
```

time: 548 us -> 234 us (0.43); the launches traced: 538 us -> 234 us
  Pallas kernels: 0 us -> 222 us
  waiting for transfers between devices: 192 us -> 0 us
  blocking collectives: 172 us -> 0 us
  matrix products: 74.5 us -> 0 us
  local copies, waits for them, and re-layouts: 52.1 us -> 9.03 us
  other arithmetic: 25.8 us -> 2.12 us
  starting transfers between devices: 21.1 us -> 0 us
    pallas_call x0 -> x1, Pallas kernels: none -> 222 us  [body(): pl.pallas_call(functools.partial(sweep, side, order), out_shape=jax.Shape...]
    all_to_all x3 -> x0, blocking collectives: 172 us -> none  [body(): lax.all_to_all(prod[slot_index] * slot_used[:, None, None], 'trace', spli...]
    all_to_all x2 -> x0, waiting for transfers between devices: 96.3 us -> none  [body(): lax.all_to_all(prod[slot_index] * slot_used[:, None, None], 'trace', spli...]
    ppermute x4 -> x0, waiting for transfers between devices: 95.7 us -> none  [passed_along(): lax.ppermute(value, axis, [(source, source + steps) for source in range(i...]
    dot_general x10 -> x0, matrix products: 74.5 us -> none  [the longest x5 57.4 us: body(): jnp.einsum('kij,kjc->kic', blocks, pieces, preferred_element_type=jnp.flo...]
    gather x10 -> x0, local copies, waits for them, and re-layouts: 28.7 us -> none  [the longest x5 15.2 us: body(): prod[slot_index] * slot_used[:, None, None]]
    convert_element_type x10 -> x0, local copies, waits for them, and re-layouts: 18.1 us -> none  [the longest x5 17.4 us: body(): prod = jnp.einsum('kij,kjc->kic', blocks, pieces, preferred_element_type=...]
    mul x5 -> x0, other arithmetic: 16.6 us -> none  [body(): prod[slot_index] * slot_used[:, None, None]]
  transfers between devices with their start and end apart: 6 -> 0, of which waited for: 6 -> 0; matrix products, arithmetic and copies ran while one was open for 1% -> 0% of each run, Pallas kernels for 0% -> 0%
where the time goes in v1:
time: 234 us
  Pallas kernels  222 us (95%)
  local copies, waits for them, and re-layouts  9.03 us (4%)
    pallas_call x1, Pallas kernels, body(): pl.pallas_call(functools.partial(sweep, side, order), out_shape=jax.Shape...  222 us

profile of v1, /device:TPU:7, one launch (start us, length us, event | category | flops | bytes accessed | tf_op | source)
XLA Modules:
  0.0 233.5 jit_solution(17073163756683976048)
XLA Ops:
  0.0 0.7 fusion.3
  0.7 0.9 dynamic-slice_reduce_fusion
  1.6 0.7 subtract_bitcast_fusion
  2.3 0.1 select_reduce_fusion.1
  2.4 0.6 pad_add_fusion.table
  3.0 4.1 %copy.7 = bf16[2,128,4096]{2,1,0:T(8,128)(2,1)} copy(bf16[2,128,4096]{1,2,0:T(8,128)(2,1)} %bitcast.36) | data formatting | bytes 4194304 | tf_op jit(solution)/shard_map/transpose | solution.py:166
  7.1 222.3 %sweep.1 = bf16[16,16,4096]{2,1,0:T(8,128)(2,1)} custom-call(s32[3,32]{1,0:T(4,128)} %pad_add_fusion.table, bf16[24,512,512]{2,1,0:T(8,128)(2,1)} %bitcast.33, bf16[16,16,4096]{2,1,0:T(8,128)(2,1)} %bitcast.35), custom_call_target="tpu_custom_call" | custom-call | tf_op jit(solution)/shard_map/sweep/pallas_call | solution.py:168
  229.4 4.1 %copy.8 = bf16[2,128,4096]{1,2,0:T(8,128)(2,1)} copy(bf16[2,128,4096]{2,1,0:T(8,128)(2,1)} %bitcast.34) | data formatting | bytes 4194304 | tf_op jit(solution)/shard_map/reshape | solution.py:194
  (2 shorter events, 0.0 us)

commit v2 on v1

v2 whole, which is shorter than its diff:
```python
import functools

import jax
import jax.numpy as jnp
from jax import lax
from jax.experimental import pallas as pl
from jax.experimental.pallas import tpu as pltpu
from jax.sharding import PartitionSpec as P

MESH = pl.DeviceIdType.MESH
CHUNK = 16
PIECES = 4
LOADS = 6
RING = 4
GROUP = 4


def displacements(senders):
    side = 4 if senders == 32 else 2
    if side == 2:
        kinds = [[(1, 1)], [(1, 0), (0, 1)]]
    else:
        kinds = [
            [(2, 2)],
            [(2, 1), (1, 2), (2, 3), (3, 2)],
            [(1, 1), (3, 1), (3, 3), (1, 3)],
            [(2, 0), (0, 2)],
            [(1, 0), (0, 1), (3, 0), (0, 3)],
        ]
    order = [(a, b, core) for alike in kinds for core in range(2) for a, b in alike]
    return side, order + [(0, 0, 1)]


def sweep(
    side, order, row_block, col_block, operators, sources, result,
    raw, blocks, given, turned, field, sent, got, incoming, out, final, table_v, table,
    load_sem, given_sem, table_sem, result_sem, send_sem, recv_sem, down_sem, arrive_sem,
):
    chunks, wide, rows = incoming.shape
    stored, width, _ = blocks.shape
    batches, _, shots = given.shape
    each = chunks // batches
    owned = rows // width
    peers = len(order)
    part = owned // PIECES
    per_load = stored // LOADS
    depth = lax.axis_index("layer")
    layers = lax.axis_size("layer")
    me = lax.axis_index("trace")
    z, y, core = me // (2 * side), (me // 2) % side, me % 2

    def at(step, sign):
        a, b, c = step
        return ((z + sign * a + side) % side) * (2 * side) + ((y + sign * b + side) % side) * 2 + (core + c) % 2

    loads = [
        pltpu.make_async_copy(
            operators.at[pl.ds(g * per_load, per_load)], raw.at[pl.ds(g * per_load, per_load)], load_sem.at[g]
        )
        for g in range(LOADS)
    ]
    takes = [pltpu.make_async_copy(sources.at[b], given.at[b], given_sem.at[b]) for b in range(batches)]
    takes[0].start()
    for load in loads:
        load.start()
    for take in takes[1:]:
        take.start()
    barrier = pltpu.get_barrier_semaphore()
    for step in order:
        pl.semaphore_signal(barrier, inc=1, device_id=(depth, at(step, -1)), device_id_type=MESH)
    pl.semaphore_signal(
        barrier, inc=1, device_id=(lax.rem(depth + layers - 1, layers), me), device_id_type=MESH
    )

    every = row_block[...]
    mine = row_block[pl.ds(me, 1), :]
    senders = every.shape[0]
    owner = lax.broadcasted_iota(jnp.int32, every.shape, 0)
    match = jnp.broadcast_to(mine // owned, every.shape) == owner
    order_of = lax.broadcasted_iota(jnp.int32, every.shape, 1)
    near = jnp.broadcast_to(col_block[...] % owned, every.shape)
    slot = jnp.max(jnp.where(match, order_of, 0), axis=1, keepdims=True)
    column = jnp.max(jnp.where(match, near, 0), axis=1, keepdims=True)
    local = jnp.max(jnp.where(every // owned == me, every % owned + 1, 0), axis=1, keepdims=True) - 1
    lane = lax.broadcasted_iota(jnp.int32, table_v.shape, 1)
    table_v[...] = jnp.where(lane == 0, slot, jnp.where(lane == 1, column, local))
    to_scalars = pltpu.make_async_copy(table_v, table, table_sem)
    to_scalars.start()

    def turn_sources(b):
        for r in range(owned):
            span = pl.ds(r * width, width)
            turned[b, :, span] = given[b, span, :].T

    takes[0].wait()
    turn_sources(0)
    for g in range(LOADS):
        loads[g].wait()

        def flip(j, _):
            blocks[j] = raw[j].T
            return 0

        lax.fori_loop(g * per_load, (g + 1) * per_load, flip, 0)
    to_scalars.wait()
    for take in takes[1:]:
        take.wait()
    pl.semaphore_wait(barrier, peers + 1)

    def to_peer(k, i):
        return pltpu.make_async_remote_copy(
            src_ref=sent.at[k % RING, i], dst_ref=got.at[k, i], send_sem=send_sem.at[k], recv_sem=recv_sem.at[k],
            device_id=(depth, at(order[i], 1)), device_id_type=MESH,
        )

    def all_peers(k):
        return pltpu.make_async_remote_copy(
            src_ref=sent.at[k % RING], dst_ref=got.at[k, pl.ds(0, peers)], send_sem=send_sem.at[k],
            recv_sem=recv_sem.at[k], device_id=(depth, at(order[0], 1)), device_id_type=MESH,
        )

    def down(k, p):
        span = pl.ds(p * part * width, part * width)
        return pltpu.make_async_remote_copy(
            src_ref=out.at[k, :, span], dst_ref=incoming.at[k, :, span], send_sem=down_sem.at[k, p],
            recv_sem=arrive_sem.at[k, p], device_id=(lax.rem(depth + 1, layers), me), device_id_type=MESH,
        )

    def multiply(k):
        @pl.when(k >= RING)
        def _():
            all_peers(k - RING).wait_send()

        for b in range(1, batches):

            @pl.when(k == (b - 1) * each + 1)
            def _():
                turn_sources(b)

        shot = pl.ds(pl.multiple_of((k % each) * wide, wide), wide)
        for p in range(PIECES):

            @pl.when(depth > 0)
            def _():
                down(k, p).wait_recv()

            for c in range(p * part, (p + 1) * part):
                span = pl.ds(c * width, width)
                above = jnp.where(depth > 0, incoming[k, :, span].astype(jnp.float32), 0.0)
                field[c] = (above + turned[k // each, shot, span].astype(jnp.float32)).astype(jnp.bfloat16)
        for first in range(0, peers + 1, GROUP):
            span = range(first, min(first + GROUP, peers + 1))
            for i in span:
                owner = at(order[i], 1) if i < peers else me
                product = jnp.dot(
                    field[table[owner, 1]], blocks[table[owner, 0]], preferred_element_type=jnp.float32
                ).astype(jnp.bfloat16)
                if i < peers:
                    sent[k % RING, i] = product
                else:
                    got[k, i] = product
            for i in span:
                if i < peers:
                    to_peer(k, i).start()

    def collect(k):
        all_peers(k).wait_recv()
        local = [table[at(order[i], -1) if i < peers else me, 2] for i in range(peers + 1)]
        for p in range(PIECES):
            spread = range(p * part, (p + 1) * part)
            totals = [jnp.zeros((wide, width), jnp.float32) for _ in spread]
            for i in range(peers + 1):
                value = got[k, i].astype(jnp.float32)
                for n, r in enumerate(spread):
                    totals[n] += value * jnp.where(local[i] == r, 1.0, 0.0)
            for n, r in enumerate(spread):
                out[k, :, pl.ds(r * width, width)] = totals[n].astype(jnp.bfloat16)

            @pl.when(depth < layers - 1)
            def _():
                down(k, p).start()

    def hand_over(b):
        for r in range(owned):
            span = pl.ds(r * width, width)
            shots_all = out[pl.ds(b * each, each), :, span].reshape(shots, width)
            final[b, span, :] = shots_all.T
            pltpu.make_async_copy(final.at[b, span], result.at[b, span], result_sem.at[b]).start()

    def turn(k, _):
        @pl.when(k < chunks)
        def _():
            multiply(k)

        @pl.when(k > 0)
        def _():
            collect(k - 1)

        for b in range(batches):

            @pl.when(k == (b + 1) * each)
            def _():
                hand_over(b)

        return 0

    lax.fori_loop(0, chunks + 1, turn, 0)

    def finish(k, _):
        @pl.when(k >= chunks - RING)
        def _():
            all_peers(k).wait_send()

        @pl.when(depth < layers - 1)
        def _():
            for p in range(PIECES):
                down(k, p).wait_send()

        return 0

    lax.fori_loop(0, chunks, finish, 0)
    for b in range(batches):
        pltpu.make_async_copy(final.at[b], result.at[b], result_sem.at[b]).wait()


def body(operators, sources, row_block, col_block):
    senders = lax.axis_size("trace")
    _, stored, width, _ = operators.shape
    batches, rows, shots = sources.shape[1:]
    owned = rows // width
    side, order = displacements(senders)
    chunks = batches * shots // CHUNK
    peers = len(order)
    result = pl.pallas_call(
        functools.partial(sweep, side, order),
        out_shape=jax.ShapeDtypeStruct((batches, rows, shots), jnp.bfloat16),
        in_specs=[
            pl.BlockSpec(memory_space=pltpu.VMEM),
            pl.BlockSpec(memory_space=pltpu.VMEM),
            pl.BlockSpec(memory_space=pl.ANY),
            pl.BlockSpec(memory_space=pl.ANY),
        ],
        out_specs=pl.BlockSpec(memory_space=pl.ANY),
        scratch_shapes=[
            pltpu.VMEM((stored, width, width), jnp.bfloat16),
            pltpu.VMEM((stored, width, width), jnp.bfloat16),
            pltpu.VMEM((batches, rows, shots), jnp.bfloat16),
            pltpu.VMEM((batches, shots, rows), jnp.bfloat16),
            pltpu.VMEM((owned, CHUNK, width), jnp.bfloat16),
            pltpu.VMEM((RING, peers, CHUNK, width), jnp.bfloat16),
            pltpu.VMEM((chunks, peers + 1, CHUNK, width), jnp.bfloat16),
            pltpu.VMEM((chunks, CHUNK, rows), jnp.bfloat16),
            pltpu.VMEM((chunks, CHUNK, rows), jnp.bfloat16),
            pltpu.VMEM((batches, rows, shots), jnp.bfloat16),
            pltpu.VMEM((senders, 128), jnp.int32),
            pltpu.SMEM((senders, 128), jnp.int32),
            pltpu.SemaphoreType.DMA((LOADS,)),
            pltpu.SemaphoreType.DMA((batches,)),
            pltpu.SemaphoreType.DMA,
            pltpu.SemaphoreType.DMA((batches,)),
            pltpu.SemaphoreType.DMA((chunks,)),
            pltpu.SemaphoreType.DMA((chunks,)),
            pltpu.SemaphoreType.DMA((chunks, PIECES)),
            pltpu.SemaphoreType.DMA((chunks, PIECES)),
        ],
        compiler_params=pltpu.CompilerParams(
            collective_id=0, has_side_effects=True, vmem_limit_bytes=58 * 1024 * 1024
        ),
        name="sweep",
    )(row_block[0], col_block[0], operators[0], sources[0])
    return result[None]


def solution(mesh):
    placed = (
        P("layer", "trace", None, None),
        P("layer", None, "trace", None),
        P("layer", None, None),
        P("layer", "trace", None),
    )
    return jax.shard_map(
        body, mesh=mesh, in_specs=placed, out_specs=P("layer", None, "trace", None), check_vma=False
    )
```

time: 234 us -> 176 us (0.75)
  Pallas kernels: 222 us -> 171 us
  local copies, waits for them, and re-layouts: 9.03 us -> 4.43 us
    pallas_call x1, Pallas kernels: 222 us -> 171 us  [body(): pl.pallas_call(functools.partial(sweep, side, order), out_shape=jax.Shape...]
    unnamed x0 -> x2, local copies, waits for them, and re-layouts: none -> 4.43 us
    reshape x1 -> x0, local copies, waits for them, and re-layouts: 4.07 us -> none  [body(): return jnp.swapaxes(result.reshape(batches, shots, rows), 1, 2)[None]]
    transpose x1 -> x0, local copies, waits for them, and re-layouts: 4.07 us -> none  [body(): turned = jnp.swapaxes(sources[0], 1, 2).reshape(chunks, CHUNK, rows)]
where the time goes in v2:
time: 176 us
  Pallas kernels  171 us (97%)
  local copies, waits for them, and re-layouts  4.43 us (3%)
    pallas_call x1, Pallas kernels, body(): pl.pallas_call(functools.partial(sweep, side, order), out_shape=jax.Shape...  171 us
    unnamed x2, local copies, waits for them, and re-layouts  4.43 us

profile of v2, /device:TPU:7, one launch (start us, length us, event | category | flops | bytes accessed | tf_op | source)
XLA Modules:
  0.0 175.7 jit_solution(18367040713190837138)
XLA Ops:
  0.0 1.4 copy.5
  1.4 171.2 %sweep.1 = bf16[2,4096,128]{2,1,0:T(8,128)(2,1)} custom-call(s32[32,24]{1,0:T(8,128)} %bitcast.8, s32[1,24]{1,0:T(1,128)} %bitcast.9, bf16[24,512,512]{2,1,0:T(8,128)(2,1)} %bitcast.5, bf16[2,4096,128]{2,1,0:T(8,128)(2,1)} %bitcast.7), custom_call_target="tpu_custom_call" | custom-call | tf_op jit(solution)/shard_map/sweep/pallas_call | solution.py:234
  172.6 3.0 %copy.7 = bf16[1,2,4096,128]{3,2,1,0:T(8,128)(2,1)} copy(bf16[1,2,4096,128]{3,2,1,0:T(8,128)(2,1)} %bitcast.6) | data formatting | bytes 4194304

commit v3 on v2

v3 whole, which is shorter than its diff:
```python
import functools

import jax
import jax.numpy as jnp
from jax import lax
from jax.experimental import pallas as pl
from jax.experimental.pallas import tpu as pltpu
from jax.sharding import PartitionSpec as P

MESH = pl.DeviceIdType.MESH
CHUNK = 8
PIECES = 2
LOADS = 6
RING = 6
GROUP = 4


def displacements(senders):
    side = 4 if senders == 32 else 2
    if side == 2:
        kinds = [[(1, 1)], [(1, 0), (0, 1)]]
    else:
        kinds = [
            [(2, 2)],
            [(2, 1), (1, 2), (2, 3), (3, 2)],
            [(1, 1), (3, 1), (3, 3), (1, 3)],
            [(2, 0), (0, 2)],
            [(1, 0), (0, 1), (3, 0), (0, 3)],
        ]
    order = [(a, b, core) for alike in kinds for core in range(2) for a, b in alike]
    return side, order + [(0, 0, 1)]


def fold(values):
    half = values.shape[1] // 2
    return jnp.concatenate([values[:, :half], values[:, half:]], axis=0)


def unfold(values):
    half = values.shape[0] // 2
    return jnp.concatenate([values[:half], values[half:]], axis=1)


def sweep(
    side, order, row_block, col_block, operators, sources, result,
    raw, blocks, turned, field, products, sent, got, incoming, out, whole, table_v, table,
    load_sem, table_sem, send_sem, recv_sem, down_sem, arrive_sem,
):
    chunks = incoming.shape[0]
    stored, width, _ = blocks.shape
    batches, rows, shots = sources.shape
    wide = batches * shots // chunks
    half = width // 2
    each = chunks // batches
    owned = rows // width
    peers = len(order)
    part = owned // PIECES
    per_load = stored // LOADS
    depth = lax.axis_index("layer")
    layers = lax.axis_size("layer")
    me = lax.axis_index("trace")
    z, y, core = me // (2 * side), (me // 2) % side, me % 2

    def at(step, sign):
        a, b, c = step
        return ((z + sign * a + side) % side) * (2 * side) + ((y + sign * b + side) % side) * 2 + (core + c) % 2

    loads = [
        pltpu.make_async_copy(
            operators.at[pl.ds(g * per_load, per_load)], raw.at[pl.ds(g * per_load, per_load)], load_sem.at[g]
        )
        for g in range(LOADS)
    ]
    for load in loads:
        load.start()
    barrier = pltpu.get_barrier_semaphore()
    for step in order:
        pl.semaphore_signal(barrier, inc=1, device_id=(depth, at(step, -1)), device_id_type=MESH)
    pl.semaphore_signal(
        barrier, inc=1, device_id=(lax.rem(depth + layers - 1, layers), me), device_id_type=MESH
    )

    every = row_block[...]
    shape = every.shape
    place = lax.broadcasted_iota(jnp.int32, shape, 0)
    index = lax.broadcasted_iota(jnp.int32, shape, 1)
    mine = jnp.sum(jnp.where(index == me, every, 0), axis=1, keepdims=True)
    square = (stored, stored)
    diagonal = lax.broadcasted_iota(jnp.int32, square, 0) == lax.broadcasted_iota(jnp.int32, square, 1)
    near = jnp.sum(jnp.where(diagonal, col_block[...] % owned, 0), axis=1, keepdims=True)
    match = mine // owned == index
    slot = jnp.max(jnp.where(match, place, 0), axis=0, keepdims=True)
    column = jnp.max(jnp.where(match, near, 0), axis=0, keepdims=True)
    local = jnp.max(jnp.where(every // owned == me, every % owned + 1, 0), axis=0, keepdims=True) - 1
    table_v[0:1, 0 : shape[1]] = slot
    table_v[1:2, 0 : shape[1]] = column
    table_v[2:3, 0 : shape[1]] = local
    table_v[3:4, 0:stored] = col_block[...] % owned
    to_scalars = pltpu.make_async_copy(table_v, table, table_sem)
    to_scalars.start()

    def turn_sources(b):
        for r in range(owned):
            span = pl.ds(r * width, width)
            turned[b, :, span] = sources[b, span, :].astype(jnp.float32).T

    turn_sources(0)
    for g in range(LOADS):
        loads[g].wait()

        def flip(j, _):
            blocks[j] = raw[j].T
            return 0

        lax.fori_loop(g * per_load, (g + 1) * per_load, flip, 0)
    to_scalars.wait()
    pl.semaphore_wait(barrier, peers + 1)

    def to_peer(k, i):
        return pltpu.make_async_remote_copy(
            src_ref=sent.at[k % RING, i], dst_ref=got.at[k, i], send_sem=send_sem.at[k], recv_sem=recv_sem.at[k],
            device_id=(depth, at(order[i], 1)), device_id_type=MESH,
        )

    def all_peers(k):
        return pltpu.make_async_remote_copy(
            src_ref=sent.at[k % RING], dst_ref=got.at[k, pl.ds(0, peers)], send_sem=send_sem.at[k],
            recv_sem=recv_sem.at[k], device_id=(depth, at(order[0], 1)), device_id_type=MESH,
        )

    def down(k, p):
        span = pl.ds(p * part * half, part * half)
        return pltpu.make_async_remote_copy(
            src_ref=out.at[k, :, span], dst_ref=incoming.at[k, :, span], send_sem=down_sem.at[k, p],
            recv_sem=arrive_sem.at[k, p], device_id=(lax.rem(depth + 1, layers), me), device_id_type=MESH,
        )

    def multiply(k):
        @pl.when(k >= RING)
        def _():
            all_peers(k - RING).wait_send()

        for b in range(1, batches):

            @pl.when(k == (b - 1) * each + 1)
            def _():
                turn_sources(b)

        shot = pl.ds(pl.multiple_of((k % each) * wide, wide), wide)
        for p in range(PIECES):

            @pl.when(depth > 0)
            def _():
                down(k, p).wait_recv()

            for c in range(p * part, (p + 1) * part):
                above = unfold(incoming[k, :, pl.ds(c * half, half)].astype(jnp.float32))
                tile = jnp.where(depth > 0, above, 0.0) + turned[k // each, shot, pl.ds(c * width, width)]
                field[c] = jnp.concatenate([tile, tile], axis=0).astype(jnp.bfloat16)
        for j in range(stored):
            product = jnp.dot(field[table[3, j]], blocks[j], preferred_element_type=jnp.float32)
            products[j] = fold(product[:wide]).astype(jnp.bfloat16)
        for first in range(0, peers + 1, GROUP):
            span = range(first, min(first + GROUP, peers + 1))
            for i in span:
                owner = at(order[i], 1) if i < peers else me
                if i < peers:
                    sent[k % RING, i] = products[table[0, owner]]
                else:
                    got[k, i] = products[table[0, owner]]
            for i in span:
                if i < peers:
                    to_peer(k, i).start()

    def collect(k):
        all_peers(k).wait_recv()
        shot = pl.ds(pl.multiple_of((k % each) * wide, wide), wide)
        local = [table[2, at(order[i], -1) if i < peers else me] for i in range(peers + 1)]
        for p in range(PIECES):
            spread = range(p * part, (p + 1) * part)
            totals = [jnp.zeros((2 * wide, half), jnp.float32) for _ in spread]
            for i in range(peers + 1):
                value = got[k, i].astype(jnp.float32)
                for n, r in enumerate(spread):
                    totals[n] += value * jnp.where(local[i] == r, 1.0, 0.0)
            for n, r in enumerate(spread):
                out[k, :, pl.ds(r * half, half)] = totals[n].astype(jnp.bfloat16)
                whole[shot, pl.ds(r * width, width)] = unfold(totals[n])

            @pl.when(depth < layers - 1)
            def _():
                down(k, p).start()

    def hand_over(b):
        for r in range(owned):
            span = pl.ds(r * width, width)
            result[b, span, :] = whole[:, span].T.astype(jnp.bfloat16)

    behind = jnp.where(depth == 0, 3, 2)

    def turn(k, _):
        @pl.when(k < chunks)
        def _():
            multiply(k)

        done = k - behind

        @pl.when((done >= 0) & (done < chunks))
        def _():
            collect(done)

        for b in range(batches):

            @pl.when(done == (b + 1) * each - 1)
            def _():
                hand_over(b)

        return 0

    lax.fori_loop(0, chunks + 3, turn, 0)

    def finish(k, _):
        @pl.when(k >= chunks - RING)
        def _():
            all_peers(k).wait_send()

        @pl.when(depth < layers - 1)
        def _():
            for p in range(PIECES):
                down(k, p).wait_send()

        return 0

    lax.fori_loop(0, chunks, finish, 0)


def body(operators, sources, row_block, col_block):
    senders = lax.axis_size("trace")
    _, stored, width, _ = operators.shape
    batches, rows, shots = sources.shape[1:]
    owned = rows // width
    side, order = displacements(senders)
    chunks = batches * shots // CHUNK
    peers = len(order)
    result = pl.pallas_call(
        functools.partial(sweep, side, order),
        out_shape=jax.ShapeDtypeStruct((batches, rows, shots), jnp.bfloat16),
        in_specs=[
            pl.BlockSpec(memory_space=pltpu.VMEM),
            pl.BlockSpec(memory_space=pltpu.VMEM),
            pl.BlockSpec(memory_space=pl.ANY),
            pl.BlockSpec(memory_space=pltpu.VMEM),
        ],
        out_specs=pl.BlockSpec(memory_space=pltpu.VMEM),
        scratch_shapes=[
            pltpu.VMEM((stored, width, width), jnp.bfloat16),
            pltpu.VMEM((stored, width, width), jnp.bfloat16),
            pltpu.VMEM((batches, shots, rows), jnp.float32),
            pltpu.VMEM((owned, 2 * CHUNK, width), jnp.bfloat16),
            pltpu.VMEM((stored, 2 * CHUNK, width // 2), jnp.bfloat16),
            pltpu.VMEM((RING, peers, 2 * CHUNK, width // 2), jnp.bfloat16),
            pltpu.VMEM((chunks, peers + 1, 2 * CHUNK, width // 2), jnp.bfloat16),
            pltpu.VMEM((chunks, 2 * CHUNK, rows // 2), jnp.bfloat16),
            pltpu.VMEM((chunks, 2 * CHUNK, rows // 2), jnp.bfloat16),
            pltpu.VMEM((shots, rows), jnp.float32),
            pltpu.VMEM((8, 128), jnp.int32),
            pltpu.SMEM((8, 128), jnp.int32),
            pltpu.SemaphoreType.DMA((LOADS,)),
            pltpu.SemaphoreType.DMA,
            pltpu.SemaphoreType.DMA((chunks,)),
            pltpu.SemaphoreType.DMA((chunks,)),
            pltpu.SemaphoreType.DMA((chunks, PIECES)),
            pltpu.SemaphoreType.DMA((chunks, PIECES)),
        ],
        compiler_params=pltpu.CompilerParams(
            collective_id=0, has_side_effects=True, vmem_limit_bytes=54 * 1024 * 1024
        ),
        name="sweep",
    )(row_block[0].T, col_block[0], operators[0], sources[0])
    return result[None]


def solution(mesh):
    placed = (
        P("layer", "trace", None, None),
        P("layer", None, "trace", None),
        P("layer", None, None),
        P("layer", "trace", None),
    )
    return jax.shard_map(
        body, mesh=mesh, in_specs=placed, out_specs=P("layer", None, "trace", None), check_vma=False
    )
```

time: 176 us -> 148 us (0.84)
  Pallas kernels: 171 us -> 145 us
    pallas_call x1, Pallas kernels: 171 us -> 145 us  [body(): pl.pallas_call(functools.partial(sweep, side, order), out_shape=jax.Shape...]
    unnamed x2 -> x1, local copies, waits for them, and re-layouts: 4.43 us -> 3.05 us
where the time goes in v3:
time: 148 us
  Pallas kernels  145 us (98%)
  local copies, waits for them, and re-layouts  3.05 us (2%)
    pallas_call x1, Pallas kernels, body(): pl.pallas_call(functools.partial(sweep, side, order), out_shape=jax.Shape...  145 us
    unnamed x1, local copies, waits for them, and re-layouts  3.05 us

profile of v3, /device:TPU:7, one launch (start us, length us, event | category | flops | bytes accessed | tf_op | source)
XLA Modules:
  0.0 147.9 jit_solution(2614072727073884926)
XLA Ops:
  0.0 144.9 %sweep.1 = bf16[2,4096,128]{2,1,0:T(8,128)(2,1)} custom-call(s32[24,32]{1,0:T(8,128)} %bitcast.10, s32[1,24]{1,0:T(1,128)} %bitcast.11, bf16[24,512,512]{2,1,0:T(8,128)(2,1)} %bitcast.7, bf16[2,4096,128]{2,1,0:T(8,128)(2,1)} %bitcast.9), custom_call_target="tpu_custom_call" | custom-call | tf_op jit(solution)/shard_map/sweep/pallas_call | solution.py:245
  144.9 3.0 %copy.6 = bf16[1,2,4096,128]{3,2,1,0:T(8,128)(2,1)} copy(bf16[1,2,4096,128]{3,2,1,0:T(8,128)(2,1)} %bitcast.8) | data formatting | bytes 4194304

commit v4 on v3

--- a/solution.py
+++ b/solution.py
@@ -12,6 +12,7 @@
 PIECES = 2
 LOADS = 6
 RING = 6
+EARLY = 4
 GROUP = 4
 
 
@@ -43,7 +44,7 @@
 
 def sweep(
     side, order, row_block, col_block, operators, sources, result,
-    raw, blocks, turned, field, products, sent, got, incoming, out, whole, table_v, table,
+    raw, blocks, turned, ahead, first, field, products, sent, got, incoming, out, whole, table_v, table,
     load_sem, table_sem, send_sem, recv_sem, down_sem, arrive_sem,
 ):
     chunks = incoming.shape[0]
@@ -104,16 +105,33 @@
             span = pl.ds(r * width, width)
             turned[b, :, span] = sources[b, span, :].astype(jnp.float32).T
 
-    turn_sources(0)
-    for g in range(LOADS):
-        loads[g].wait()
-
+    def early(g):
+        for j in range(g * per_load, (g + 1) * per_load):
+            column = table[3, j]
+            product = lax.dot_general(
+                ahead[column], raw[j], (((1,), (1,)), ((), ())), preferred_element_type=jnp.float32
+            )
+            for k in range(EARLY):
+                first[k, j] = fold(product[k * wide : (k + 1) * wide]).astype(jnp.bfloat16)
+
+    def flip_all():
         def flip(j, _):
             blocks[j] = raw[j].T
             return 0
 
-        lax.fori_loop(g * per_load, (g + 1) * per_load, flip, 0)
+        lax.fori_loop(0, stored, flip, 0)
+
+    turn_sources(0)
+    for c in range(owned):
+        ahead[c] = turned[0, 0 : EARLY * wide, pl.ds(c * width, width)].astype(jnp.bfloat16)
     to_scalars.wait()
+    for g in range(LOADS):
+        loads[g].wait()
+
+        @pl.when(depth == 0)
+        def _():
+            early(g)
+
     pl.semaphore_wait(barrier, peers + 1)
 
     def to_peer(k, i):
@@ -135,6 +153,19 @@
             recv_sem=arrive_sem.at[k, p], device_id=(lax.rem(depth + 1, layers), me), device_id_type=MESH,
         )
 
+    def send(k, held):
+        for start in range(0, peers + 1, GROUP):
+            span = range(start, min(start + GROUP, peers + 1))
+            for i in span:
+                owner = at(order[i], 1) if i < peers else me
+                if i < peers:
+                    sent[k % RING, i] = held[table[0, owner]]
+                else:
+                    got[k, i] = held[table[0, owner]]
+            for i in span:
+                if i < peers:
+                    to_peer(k, i).start()
+
     def multiply(k):
         @pl.when(k >= RING)
         def _():
@@ -142,7 +173,7 @@
 
         for b in range(1, batches):
 
-            @pl.when(k == (b - 1) * each + 1)
+            @pl.when(k == (b - 1) * each + EARLY + 1)
             def _():
                 turn_sources(b)
 
@@ -160,17 +191,7 @@
         for j in range(stored):
             product = jnp.dot(field[table[3, j]], blocks[j], preferred_element_type=jnp.float32)
             products[j] = fold(product[:wide]).astype(jnp.bfloat16)
-        for first in range(0, peers + 1, GROUP):
-            span = range(first, min(first + GROUP, peers + 1))
-            for i in span:
-                owner = at(order[i], 1) if i < peers else me
-                if i < peers:
-                    sent[k % RING, i] = products[table[0, owner]]
-                else:
-                    got[k, i] = products[table[0, owner]]
-            for i in span:
-                if i < peers:
-                    to_peer(k, i).start()
+        send(k, products)
 
     def collect(k):
         all_peers(k).wait_recv()
@@ -196,10 +217,17 @@
             span = pl.ds(r * width, width)
             result[b, span, :] = whole[:, span].T.astype(jnp.bfloat16)
 
+    @pl.when(depth == 0)
+    def _():
+        for k in range(EARLY):
+            send(k, first.at[k])
+
+    flip_all()
     behind = jnp.where(depth == 0, 3, 2)
+    begin = jnp.where(depth == 0, EARLY, 0)
 
     def turn(k, _):
-        @pl.when(k < chunks)
+        @pl.when((k < chunks) & (k >= begin))
         def _():
             multiply(k)
 
@@ -256,6 +284,8 @@
             pltpu.VMEM((stored, width, width), jnp.bfloat16),
             pltpu.VMEM((stored, width, width), jnp.bfloat16),
             pltpu.VMEM((batches, shots, rows), jnp.float32),
+            pltpu.VMEM((owned, EARLY * CHUNK, width), jnp.bfloat16),
+            pltpu.VMEM((EARLY, stored, 2 * CHUNK, width // 2), jnp.bfloat16),
             pltpu.VMEM((owned, 2 * CHUNK, width), jnp.bfloat16),
             pltpu.VMEM((stored, 2 * CHUNK, width // 2), jnp.bfloat16),
             pltpu.VMEM((RING, peers, 2 * CHUNK, width // 2), jnp.bfloat16),
@@ -273,7 +303,7 @@
             pltpu.SemaphoreType.DMA((chunks, PIECES)),
         ],
         compiler_params=pltpu.CompilerParams(
-            collective_id=0, has_side_effects=True, vmem_limit_bytes=54 * 1024 * 1024
+            collective_id=0, has_side_effects=True, vmem_limit_bytes=50 * 1024 * 1024
         ),
         name="sweep",
     )(row_block[0].T, col_block[0], operators[0], sources[0])

time: 148 us -> 144 us (0.973)
  Pallas kernels: 145 us -> 141 us
    pallas_call x1, Pallas kernels: 145 us -> 141 us  [body(): pl.pallas_call(functools.partial(sweep, side, order), out_shape=jax.Shape...]
    unnamed x1 -> x5, local copies, waits for them, and re-layouts: 3.05 us -> 2.68 us
where the time goes in v4:
time: 144 us
  Pallas kernels  141 us (98%)
  local copies, waits for them, and re-layouts  2.68 us (2%)
    pallas_call x1, Pallas kernels, body(): pl.pallas_call(functools.partial(sweep, side, order), out_shape=jax.Shape...  141 us

profile of v4, /device:TPU:7, one launch (start us, length us, event | category | flops | bytes accessed | tf_op | source)
XLA Modules:
  0.0 143.5 jit_solution(13242020599004633455)
XLA Ops:
  0.0 0.0 copy-start
  0.0 0.7 copy-done
  0.7 0.0 copy-start.1
  0.7 0.7 copy-done.1
  1.4 140.9 %sweep.1 = bf16[2,4096,128]{2,1,0:T(8,128)(2,1)S(1)} custom-call(s32[24,32]{1,0:T(8,128)S(1)} %bitcast.8, s32[1,24]{1,0:T(1,128)S(1)} %bitcast.9, bf16[24,512,512]{2,1,0:T(8,128)(2,1)} %bitcast.10, bf16[2,4096,128]{2,1,0:T(8,128)(2,1)} %bitcast.11), custom_call_target="tpu_custom_call" | custom-call | tf_op jit(solution)/shard_map/sweep/pallas_call | solution.py:273
  142.2 1.3 copy.6
Async XLA Ops:
  0.0 0.7 copy-start
  0.7 0.7 copy-start.1

commit v5 on v4

--- a/solution.py
+++ b/solution.py
@@ -9,7 +9,7 @@
 
 MESH = pl.DeviceIdType.MESH
 CHUNK = 8
-PIECES = 2
+PIECES = 1
 LOADS = 6
 RING = 6
 EARLY = 4

time: 144 us -> 144 us (level)
  no operation moved by 1% of the time
where the time goes in v5:
time: 144 us
  Pallas kernels  141 us (98%)
  local copies, waits for them, and re-layouts  2.68 us (2%)
    pallas_call x1, Pallas kernels, body(): pl.pallas_call(functools.partial(sweep, side, order), out_shape=jax.Shape...  141 us

profile of v5, /device:TPU:7, one launch (start us, length us, event | category | flops | bytes accessed | tf_op | source)
XLA Modules:
  0.0 144.0 jit_solution(11107527911344000637)
XLA Ops:
  0.0 0.0 copy-start
  0.0 0.7 copy-done
  0.7 0.0 copy-start.1
  0.7 0.7 copy-done.1
  1.4 141.4 %sweep.1 = bf16[2,4096,128]{2,1,0:T(8,128)(2,1)S(1)} custom-call(s32[24,32]{1,0:T(8,128)S(1)} %bitcast.8, s32[1,24]{1,0:T(1,128)S(1)} %bitcast.9, bf16[24,512,512]{2,1,0:T(8,128)(2,1)} %bitcast.10, bf16[2,4096,128]{2,1,0:T(8,128)(2,1)} %bitcast.11), custom_call_target="tpu_custom_call" | custom-call | tf_op jit(solution)/shard_map/sweep/pallas_call | solution.py:273
  142.7 1.3 copy.6
Async XLA Ops:
  0.0 0.7 copy-start
  0.7 0.7 copy-start.1
